TPU v7x, 32 devices: a whole 2x2x4 slice. The times are simulated.
32 devices in a mesh: groups: 2 (over y), ctx: 4 (over x, core), head: 4 (over z).
Axes of the slice: x: 2, y: 2, z: 4, core: 2. Of those that a mesh axis runs over, the one named last changes fastest.
Arguments:
- queries: bfloat16 [12288, 512], P(('groups', 'ctx', 'head')), parts along dimension 0, may hold values from -8 to 8
- keys: bfloat16 [12288, 512], P(('groups', 'ctx', 'head')), parts along dimension 0, may hold values from -8 to 8
- values: bfloat16 [12288, 512], P(('groups', 'ctx', 'head')), parts along dimension 0, may hold values from -6 to 6
- tile_lists: int32 [96, 16], P(('groups', 'ctx')), parts along dimension 0, may hold values from -8 to 54, as said below
- live_counts: int32 [96], P(('groups', 'ctx')), parts along dimension 0, may hold values from 8 to 16
Outputs:
- attended: bfloat16 [12288, 512], P(('groups', 'ctx', 'head')), parts along dimension 0
There are 2 independent parts, one for each index of `groups`. A program takes and returns all parts, laid end to end along the dimension named above; each array names one. Nothing has to cross between parts.
Inputs may be any that keep to these rules, and one draw needn't show every extreme that they name: `tile_lists`: row t holds t + o for each offset o from -8 to 7 exactly once, the first entry being t itself; entries outside 0 to 47 occur only near the ends of the video.
All inputs are finite; a program needn't handle non-finite values.
Results may differ from a plain program's by a relative error of at most 0.0047.
Values may be sent and summed in bfloat16 or wider, within the bound.
A program may use at most 64 MiB of HBM per device.

v0:
```python
import jax
import jax.numpy as jnp
from jax import lax
from jax.sharding import PartitionSpec as P

HDIM = 128
TILE = 128
EDGE = 8
CTX_TILES = 12
LIST = 16


def with_halo(block, sides, width):
    for axis, dim in sides:
        count = lax.axis_size(axis)
        forward = [(i, i + 1) for i in range(count - 1)]
        backward = [(target, source) for source, target in forward]
        low = lax.ppermute(
            lax.slice_in_dim(block, block.shape[dim] - width, None, axis=dim), axis, forward
        )
        high = lax.ppermute(lax.slice_in_dim(block, 0, width, axis=dim), axis, backward)
        block = jnp.concatenate([low, block, high], axis=dim)
    return block


def block_tiles():
    for candidate in (4, 2, 1):
        return candidate
    return 1


def edge_tiles(kv_pair):
    return with_halo(kv_pair, (("ctx", 1),), EDGE * TILE)


def attend(q_rows, row_lists, row_counts, kv_tiles, query_first, kv_first, total_tiles):
    tile_count = row_lists.shape[0]
    per_block = block_tiles()
    block_count = tile_count // per_block
    window_span = per_block + 2 * EDGE - 1
    score_scale = HDIM ** (-0.5)
    q_blocks = q_rows.reshape(block_count, per_block, TILE, HDIM)
    block_list_entries = row_lists.reshape(block_count, per_block, LIST)
    count_blocks = row_counts.reshape(block_count, per_block)
    block_numbers = jnp.arange(block_count, dtype=jnp.int32)
    positions = jnp.arange(LIST)
    window_steps = jnp.arange(window_span, dtype=jnp.int32)

    def one_block(inputs):
        query_portion, list_part, count_part, block_number = inputs
        block_first = query_first + block_number * per_block
        window_first = block_first - EDGE
        window = lax.dynamic_slice_in_dim(kv_tiles, window_first - kv_first, window_span, 1)
        key_window_tiles = window[0].reshape(window_span * TILE, HDIM)
        value_window_tiles = window[1].reshape(window_span * TILE, HDIM)
        window_ids = window_first + window_steps
        in_range = (window_ids >= 0) & (window_ids < total_tiles)
        live = positions[None, :] < count_part[:, None]
        matched = (list_part[:, :, None] == window_ids[None, None, :]) & live[:, :, None]
        usable = jnp.any(matched, axis=1) & in_range[None, :]
        visible = jnp.repeat(usable, TILE, axis=1)[:, None, :]
        scores = (
            jnp.einsum(
                "tfy,vy->tfv", query_portion, key_window_tiles, preferred_element_type=jnp.float32
            )
            * score_scale
        )
        scores = jnp.where(visible, scores, -1e30)
        highest = jnp.max(scores, axis=-1, keepdims=True)
        weights = jnp.where(visible, jnp.exp(scores - highest), 0.0)
        softmax_divisor = jnp.sum(weights, axis=-1, keepdims=True)
        attention_probs = weights.astype(jnp.bfloat16)
        mixed = jnp.einsum(
            "jzn,nw->jzw", attention_probs, value_window_tiles, preferred_element_type=jnp.float32
        )
        return (mixed / softmax_divisor).astype(jnp.bfloat16)

    results = lax.map(one_block, (q_blocks, block_list_entries, count_blocks, block_numbers))
    return results.reshape(tile_count * TILE, HDIM)


def on_device(queries, keys, values, tile_lists, live_counts):
    ctx_count = lax.axis_size("ctx")
    total_tiles = CTX_TILES * ctx_count
    first_tile = lax.axis_index("ctx") * CTX_TILES
    kv_pair = lax.all_to_all(
        jnp.stack([keys, values]), "head", split_axis=2, concat_axis=1, tiled=True
    )
    padded = edge_tiles(kv_pair)
    local_q = lax.all_to_all(queries, "head", split_axis=1, concat_axis=0, tiled=True)
    padded_count = CTX_TILES + 2 * EDGE
    padded_tiles = padded.reshape(2, padded_count, TILE, HDIM)
    head_out = attend(
        local_q, tile_lists, live_counts, padded_tiles, first_tile, first_tile - EDGE, total_tiles
    )
    return lax.all_to_all(head_out, "head", split_axis=0, concat_axis=1, tiled=True)


def solution(mesh):
    return jax.shard_map(
        on_device,
        mesh=mesh,
        in_specs=(
            P(("groups", "ctx", "head"), None),
            P(("groups", "ctx", "head"), None),
            P(("groups", "ctx", "head"), None),
            P(("groups", "ctx"), None),
            P(("groups", "ctx")),
        ),
        out_specs=P(("groups", "ctx", "head"), None),
        check_vma=False,
    )
```

profile of v0, /device:TPU:0, one launch (start us, length us, event | category | flops | bytes accessed | tf_op | source)
XLA Modules:
  0.0 94.4 jit_solution(12368793994641363082)
XLA Ops:
  0.0 0.0 copy-start
  0.0 1.2 %pad_maximum_fusion.1 = bf16[2,384,512]{2,1,0:T(8,128)(2,1)S(1)} fusion(bf16[1,384,512]{2,1,0:T(8,128)(2,1)} %bitcast.91, bf16[1,384,512]{2,1,0:T(8,128)(2,1)} %bitcast.92), kind=kLoop, calls=%fused_computation.40 | loop fusion | flops 393216 | bytes 1572864 | tf_op jit(solution)/shard_map/stack | solution.py:87
  1.2 1.1 %copy.26 = bf16[2,384,512]{1,0,2:T(2,128)(2,1)S(1)} copy(bf16[2,384,512]{2,1,0:T(8,128)(2,1)S(1)} %pad_maximum_fusion.1) | data formatting | bytes 1572864 | tf_op jit(solution)/shard_map/stack | solution.py:87
  2.4 26.2 %all_to_all.53 = bf16[2,384,512]{1,0,2:T(2,128)(2,1)S(1)} all-to-all(bf16[2,384,512]{1,0,2:T(2,128)(2,1)S(1)} %copy.26), channel_id=1, replica_groups=mesh['groups'=2,'ctx'=4,'head'=4] {'head'}, dimensions={2} | all-to-all | bytes 1572864 | tf_op jit(solution)/shard_map/all_to_all | solution.py:86
  28.6 0.1 copy.27
  28.7 0.4 copy.28
  29.1 0.0 copy-start.1
  29.1 0.0 copy-start.2
  29.1 0.1 fusion.52
  29.2 1.3 %collective-permute-start = (bf16[2,1024,128]{2,1,0:T(8,128)(2,1)S(1)}, bf16[2,1024,128]{2,1,0:T(8,128)(2,1)S(1)}, u32[]{:S(2)}, u32[]{:S(2)}) collective-permute-start(bf16[2,1024,128]{2,1,0:T(8,128)(2,1)S(1)} %get-tuple-element.184), channel_id=1, source_target_pairs={{0,4},{4,8},{8,12},{1,5},{5,9},{9,13},{2,6},{6,10},{10,14},{3,7},{... | collective-permute-start | bytes 1572872 | tf_op jit(solution)/shard_map/ppermute | solution.py:18
  30.5 1.3 %collective-permute-start.1 = (bf16[2,1024,128]{2,1,0:T(8,128)(2,1)S(1)}, bf16[2,1024,128]{2,1,0:T(8,128)(2,1)}, u32[]{:S(2)}, u32[]{:S(2)}) collective-permute-start(bf16[2,1024,128]{2,1,0:T(8,128)(2,1)S(1)} %get-tuple-element.185), channel_id=1, source_target_pairs={{4,0},{8,4},{12,8},{5,1},{9,5},{13,9},{6,2},{10,6},{14,10},{7,3},{... | collective-permute-start | bytes 1572872 | tf_op jit(solution)/shard_map/ppermute | solution.py:21
  31.8 0.0 copy-done
  31.8 0.8 copy_bitcast_fusion.1
  32.7 4.1 %all-to-all-start = ((bf16[384,4,128]{2,0,1:T(8,128)(2,1)}), bf16[384,4,128]{2,0,1:T(8,128)(2,1)}, u32[]{:S(2)}, u32[]{:S(2)}) async-start(bf16[384,4,128]{2,0,1:T(8,128)(2,1)} %copy_bitcast_fusion.1), calls=%async_computation | async-start | bytes 786432 | tf_op jit(solution)/shard_map/all_to_all | solution.py:90
  36.8 0.0 copy-done.1
  36.8 0.0 copy-done.2
  36.8 0.1 reshape.75
  36.9 0.0 collective-permute-done
  36.9 0.0 collective-permute-done.1
  36.9 1.2 %pad_maximum_fusion = bf16[2,3584,128]{2,1,0:T(8,128)(2,1)S(1)} fusion(bf16[2,1024,128]{2,1,0:T(8,128)(2,1)} %collective-permute-done.1, bf16[2,1536,128]{2,1,0:T(8,128)(2,1)S(1)} %bitcast.87, bf16[2,1024,128]{2,1,0:T(8,128)(2,1)S(1)} %collective-permute-done), kind=kLoop, calls=%fused_computation.39 | loop fusion | flops 5505024 | bytes 3670016 | tf_op jit(solution)/shard_map/concatenate | solution.py:22
  38.1 9.7 %all-to-all-done = bf16[384,4,128]{2,0,1:T(8,128)(2,1)} async-done(((bf16[384,4,128]{2,0,1:T(8,128)(2,1)}), bf16[384,4,128]{2,0,1:T(8,128)(2,1)}, u32[]{:S(2)}, u32[]{:S(2)}) %all-to-all-start) | async-done | bytes 393248 | tf_op jit(solution)/shard_map/all_to_all | solution.py:90
  47.8 28.5 %while.13 = (s32[]{:T(128)}, bf16[3,4,128,128]{3,2,1,0:T(8,128)(2,1)}, s32[3,4,16]{2,1,0:T(4,128)S(1)}, s32[3]{0:T(128)S(1)}, s32[]{:T(128)}, /*index=5*/s32[3,4...) while((s32[]{:T(128)}, ...), condition=%wide.region_4.5_spmd.clone, body=%wide.region_0.4_spmd.clone.sunk | while | flops 968893440 | bytes 4826797 | solution.py:78
  47.8 0.6 dynamic_slice.67
  49.1 0.1 constant_dynamic-slice_fusion.4
  49.3 0.1 iota_compare_fusion.2
  49.3 0.1 and_reduce_fusion.2
  49.5 0.1 broadcast_bitcast_fusion.2
  49.6 3.1 %fusion.73 = f32[4,128]{1,0:T(4,128)S(1)} fusion(bf16[2432,128,1]{1,0,2:T(8,128)(2,1)S(1)} %bitcast.83, pred[4,2432]{1,0:T(4,128)(4,1)S(1)} %bitcast.93, bf16[3,4,128,128]{3,2,1,0:T(8,128)(2,1)} %get-tuple-element.281, s32[]{:T(128)} %get-tuple-element.260), kind=kOutput, calls=%fused_computation.42.clone.1 | convolution fusion | flops 324995456 | bytes 775680 | tf_op jit(solution)/shard_map/while/body/eval_jaxpr/sub | solution.py:70
  52.7 4.6 %fusion.74 = bf16[3,4,128,128]{3,2,1,0:T(8,128)(2,1)} fusion(bf16[3,4,128,128]{3,2,1,0:T(8,128)(2,1)} %get-tuple-element.261, s32[]{:T(128)} %get-tuple-element.260, bf16[2432,128,1]{1,0,2:T(8,128)(2,1)S(1)} %bitcast.85, f32[4,128]{1,0:T(4,128)S(1)} %fusion.73, pred[4,2432]{1,0:T(4,128)(4,1)S(1)} %bitcast.94, ...), kind=kOutput, calls=%fused_computation.12.clone.1 | convolution fusion | flops 643894144 | bytes 1529856 | tf_op jit(solution)/shard_map/while/body/eval_jaxpr/jzn,nw->jzw/dot_general | solution.py:73
  57.3 0.6 dynamic_slice.67
  58.6 0.1 constant_dynamic-slice_fusion.4
  58.7 0.1 iota_compare_fusion.2
  58.8 0.1 and_reduce_fusion.2
  58.9 0.1 broadcast_bitcast_fusion.2
  59.0 3.2 %fusion.73 = f32[4,128]{1,0:T(4,128)S(1)} fusion(bf16[2432,128,1]{1,0,2:T(8,128)(2,1)S(1)} %bitcast.83, pred[4,2432]{1,0:T(4,128)(4,1)S(1)} %bitcast.93, bf16[3,4,128,128]{3,2,1,0:T(8,128)(2,1)} %get-tuple-element.281, s32[]{:T(128)} %get-tuple-element.260), kind=kOutput, calls=%fused_computation.42.clone.1 | convolution fusion | flops 324995456 | bytes 775680 | tf_op jit(solution)/shard_map/while/body/eval_jaxpr/sub | solution.py:70
  62.2 4.6 %fusion.74 = bf16[3,4,128,128]{3,2,1,0:T(8,128)(2,1)} fusion(bf16[3,4,128,128]{3,2,1,0:T(8,128)(2,1)} %get-tuple-element.261, s32[]{:T(128)} %get-tuple-element.260, bf16[2432,128,1]{1,0,2:T(8,128)(2,1)S(1)} %bitcast.85, f32[4,128]{1,0:T(4,128)S(1)} %fusion.73, pred[4,2432]{1,0:T(4,128)(4,1)S(1)} %bitcast.94, ...), kind=kOutput, calls=%fused_computation.12.clone.1 | convolution fusion | flops 643894144 | bytes 1529856 | tf_op jit(solution)/shard_map/while/body/eval_jaxpr/jzn,nw->jzw/dot_general | solution.py:73
  66.8 0.6 dynamic_slice.67
  68.0 0.1 constant_dynamic-slice_fusion.4
  68.2 0.1 iota_compare_fusion.2
  68.3 0.1 and_reduce_fusion.2
  68.4 0.1 broadcast_bitcast_fusion.2
  68.5 3.2 %fusion.73 = f32[4,128]{1,0:T(4,128)S(1)} fusion(bf16[2432,128,1]{1,0,2:T(8,128)(2,1)S(1)} %bitcast.83, pred[4,2432]{1,0:T(4,128)(4,1)S(1)} %bitcast.93, bf16[3,4,128,128]{3,2,1,0:T(8,128)(2,1)} %get-tuple-element.281, s32[]{:T(128)} %get-tuple-element.260), kind=kOutput, calls=%fused_computation.42.clone.1 | convolution fusion | flops 324995456 | bytes 775680 | tf_op jit(solution)/shard_map/while/body/eval_jaxpr/sub | solution.py:70
  71.7 4.6 %fusion.74 = bf16[3,4,128,128]{3,2,1,0:T(8,128)(2,1)} fusion(bf16[3,4,128,128]{3,2,1,0:T(8,128)(2,1)} %get-tuple-element.261, s32[]{:T(128)} %get-tuple-element.260, bf16[2432,128,1]{1,0,2:T(8,128)(2,1)S(1)} %bitcast.85, f32[4,128]{1,0:T(4,128)S(1)} %fusion.73, pred[4,2432]{1,0:T(4,128)(4,1)S(1)} %bitcast.94, ...), kind=kOutput, calls=%fused_computation.12.clone.1 | convolution fusion | flops 643894144 | bytes 1529856 | tf_op jit(solution)/shard_map/while/body/eval_jaxpr/jzn,nw->jzw/dot_general | solution.py:73
  76.3 16.9 %all_to_all.54 = bf16[4,384,128]{2,1,0:T(8,128)(2,1)S(1)} all-to-all(bf16[4,384,128]{2,1,0:T(8,128)(2,1)} %bitcast.90), channel_id=1, replica_groups=mesh['groups'=2,'ctx'=4,'head'=4] {'head'}, dimensions={0} | all-to-all | bytes 786432 | tf_op jit(solution)/shard_map/all_to_all | solution.py:96
  93.2 0.2 copy.29
  93.5 0.9 copy.30
  (21 shorter events, 0.2 us)
Async XLA Ops:
  0.0 31.8 %copy-start = (bf16[384,512]{1,0:T(8,128)(2,1)S(1)}, bf16[384,512]{1,0:T(8,128)(2,1)}, u32[]{:S(2)}) copy-start(bf16[384,512]{1,0:T(8,128)(2,1)} %param.7) | copy-start | bytes 1179652
  29.1 7.7 %copy-start.1 = (s32[12,16]{1,0:T(8,128)S(1)}, s32[12,16]{1,0:T(8,128)}, u32[]{:S(2)}) copy-start(s32[12,16]{1,0:T(8,128)} %param.10) | copy-start | bytes 2308
  29.1 7.7 %copy-start.2 = (s32[12]{0:T(128)S(1)}, s32[12]{0:T(128)}, u32[]{:S(2)}) copy-start(s32[12]{0:T(128)} %param.11) | copy-start | bytes 148
  29.2 7.7 %collective-permute-start = (bf16[2,1024,128]{2,1,0:T(8,128)(2,1)S(1)}, bf16[2,1024,128]{2,1,0:T(8,128)(2,1)S(1)}, u32[]{:S(2)}, u32[]{:S(2)}) collective-permute-start(bf16[2,1024,128]{2,1,0:T(8,128)(2,1)S(1)} %get-tuple-element.184), channel_id=1, source_target_pairs={{0,4},{4,8},{8,12},{1,5},{5,9},{9,13},{2,6},{6,10},{10,14},{3,7},{... | collective-permute-start | bytes 1572872 | tf_op jit(solution)/shard_map/ppermute | solution.py:18
  30.5 6.4 %collective-permute-start.1 = (bf16[2,1024,128]{2,1,0:T(8,128)(2,1)S(1)}, bf16[2,1024,128]{2,1,0:T(8,128)(2,1)}, u32[]{:S(2)}, u32[]{:S(2)}) collective-permute-start(bf16[2,1024,128]{2,1,0:T(8,128)(2,1)S(1)} %get-tuple-element.185), channel_id=1, source_target_pairs={{4,0},{8,4},{12,8},{5,1},{9,5},{13,9},{6,2},{10,6},{14,10},{7,3},{... | collective-permute-start | bytes 1572872 | tf_op jit(solution)/shard_map/ppermute | solution.py:21
  32.7 15.2 %all-to-all-start = ((bf16[384,4,128]{2,0,1:T(8,128)(2,1)}), bf16[384,4,128]{2,0,1:T(8,128)(2,1)}, u32[]{:S(2)}, u32[]{:S(2)}) async-start(bf16[384,4,128]{2,0,1:T(8,128)(2,1)} %copy_bitcast_fusion.1), calls=%async_computation | async-start | bytes 786432 | tf_op jit(solution)/shard_map/all_to_all | solution.py:90
where the time goes:
time: 94.9 us; the launch traced here: 94.4 us
  blocking collectives  43.2 us (46%)
  matrix products  23.3 us (25%)
  waiting for transfers between devices  9.74 us (10%)
  starting transfers between devices  6.73 us (7%)
  local copies, waits for them, and re-layouts  6.34 us (7%)
  other arithmetic  2.97 us (3%)
  loops' own time  2.05 us (2%)
    all_to_all x1, blocking collectives, on_device(): lax.all_to_all(jnp.stack([keys, values]), 'head', split_axis=2, concat_ax...  26.2 us
    all_to_all x1, blocking collectives, on_device(): lax.all_to_all(head_out, 'head', split_axis=0, concat_axis=1, tiled=True)  16.9 us
    dot_general x3, matrix products, one_block(): jnp.einsum('jzn,nw->jzw', attention_probs, value_window_tiles, preferred_...  13.8 us
    all_to_all x1, waiting for transfers between devices, on_device(): lax.all_to_all(queries, 'head', split_axis=1, concat_axis=0, tiled=True)  9.74 us
    sub x3, matrix products, one_block(): weights = jnp.where(visible, jnp.exp(scores - highest), 0.0)  9.46 us
    all_to_all x1, starting transfers between devices, on_device(): lax.all_to_all(queries, 'head', split_axis=1, concat_axis=0, tiled=True)  4.11 us
    another operation x1, loops' own time, attend(): lax.map(one_block, (q_blocks, block_list_entries, count_blocks, block_num...  2.05 us
  transfers between devices with their start and end apart: 3, of which 1 were waited for; matrix products, arithmetic and copies ran while one was open for 2% of the time, Pallas kernels for 0%

commit v1 on v0

v1 whole, which is shorter than its diff:
```python
import functools
import math

import jax
import jax.numpy as jnp
from jax import lax
from jax.experimental import pallas as pl
from jax.experimental.pallas import tpu as pltpu
from jax.sharding import PartitionSpec as P

HDIM = 128
TILE = 128
EDGE = 8
HALO = EDGE * TILE
MASKED = -1e30
MESH = pl.DeviceIdType.MESH
K, V, Q = 0, 1, 2


def partner(me, d, n):
    if n & (n - 1):
        return lax.rem(me + d, n)
    out, bit = 0, 1
    while bit < n:
        mine = lax.rem(me // bit, 2)
        flip = (d // bit) % 2
        out = out + bit * (mine + flip * (1 - 2 * mine))
        bit *= 2
    return out


def kernel(
    n, ctx_count, tiles, group,
    counts_ref, lists_ref, q_ref, k_ref, v_ref, out_ref,
    qa, ka, va, oscr, bias,
    send_sem, recv_sem, halo_send, halo_recv, o_send, o_recv, own_sem,
):
    rows = q_ref.shape[0]
    total = tiles * TILE
    me = lax.axis_index("head")
    c = lax.axis_index("ctx")
    order = sorted(range(1, n), reverse=True)

    barrier = pltpu.get_barrier_semaphore()
    for d in range(1, n):
        pl.semaphore_signal(barrier, 1, device_id={"head": partner(me, d, n)}, device_id_type=MESH)

    @pl.when(c > 0)
    def _():
        pl.semaphore_signal(barrier, 1, device_id={"ctx": c - 1}, device_id_type=MESH)

    @pl.when(c < ctx_count - 1)
    def _():
        pl.semaphore_signal(barrier, 1, device_id={"ctx": c + 1}, device_id_type=MESH)

    def columns(s):
        return pl.ds(pl.multiple_of(s * HDIM, HDIM), HDIM)

    sources = (k_ref, v_ref, q_ref)
    targets = (ka, va, qa)
    firsts = (HALO, HALO, 0)

    def landing(kind, s):
        first = firsts[kind] + s * rows
        return targets[kind].at[pl.ds(pl.multiple_of(first, 16), rows), pl.ds(0, HDIM)]

    def own(kind):
        return pltpu.make_async_copy(
            sources[kind].at[:, columns(me)], landing(kind, me), recv_sem.at[kind, me]
        )

    def send(kind, d):
        s = partner(me, d, n)
        return pltpu.make_async_remote_copy(
            src_ref=sources[kind].at[:, columns(s)],
            dst_ref=landing(kind, me),
            send_sem=send_sem.at[kind, d],
            recv_sem=recv_sem.at[kind, me],
            device_id={"head": s},
            device_id_type=MESH,
        )

    def arrived(kind, s):
        there = landing(kind, s)
        pltpu.make_async_copy(there, there, recv_sem.at[kind, s]).wait()

    @pl.when(jnp.logical_and(c > 0, c < ctx_count - 1))
    def _():
        pl.semaphore_wait(barrier, n + 1)

    @pl.when(jnp.logical_or(c == 0, c == ctx_count - 1))
    def _():
        pl.semaphore_wait(barrier, n)

    for kind in (K, V, Q):
        for d in order:
            send(kind, d).start()
        own(kind).start()

    @pl.when(c == 0)
    def _():
        ka[pl.ds(0, HALO), pl.ds(0, HDIM)] = jnp.zeros((HALO, HDIM), jnp.bfloat16)
        va[pl.ds(0, HALO), pl.ds(0, HDIM)] = jnp.zeros((HALO, HDIM), jnp.bfloat16)

    @pl.when(c == ctx_count - 1)
    def _():
        ka[pl.ds(HALO + total, HALO), pl.ds(0, HDIM)] = jnp.zeros((HALO, HDIM), jnp.bfloat16)
        va[pl.ds(HALO + total, HALO), pl.ds(0, HDIM)] = jnp.zeros((HALO, HDIM), jnp.bfloat16)

    window_tiles = tiles + 2 * EDGE
    lanes = lax.broadcasted_iota(jnp.int32, (TILE, HDIM), 1)
    for t in range(window_tiles):
        ka[pl.ds(t * TILE, TILE), pl.ds(HDIM, HDIM)] = jnp.where(lanes == t, 1.0, 0.0).astype(jnp.bfloat16)
    va[:, pl.ds(HDIM, HDIM)] = jnp.ones((window_tiles * TILE, HDIM), jnp.bfloat16)

    row = lax.broadcasted_iota(jnp.int32, (tiles, HDIM), 0)
    ids = lax.broadcasted_iota(jnp.int32, (tiles, HDIM), 1) + (c * tiles - EDGE)
    count = jnp.zeros((tiles, HDIM), jnp.int32)
    for t in range(tiles):
        count = jnp.where(row == t, counts_ref[t], count)
    entries = lists_ref[...]
    hits = jnp.zeros((tiles, HDIM), jnp.int32)
    for j in range(entries.shape[1]):
        hit = jnp.logical_and(entries[:, j : j + 1] == ids, count > j)
        hits = jnp.where(hit, 1, hits)
    inside = jnp.logical_and(ids >= 0, ids < tiles * ctx_count)
    bias[...] = jnp.where(jnp.logical_and(hits > 0, inside), 0.0, MASKED)
    for t in range(tiles):
        mask = jnp.broadcast_to(bias[pl.ds(t, 1), :], (TILE, HDIM))
        qa[pl.ds(t * TILE, TILE), pl.ds(HDIM, HDIM)] = mask.astype(jnp.bfloat16)

    def halo_copies(s):
        out = []
        low, high = max(s * rows, total - HALO), (s + 1) * rows
        if low < high:
            out.append((0, c < ctx_count - 1, c > 0, c + 1, low, low - (total - HALO), high - low))
        low, high = s * rows, min((s + 1) * rows, HALO)
        if low < high:
            out.append((1, c > 0, c < ctx_count - 1, c - 1, low, HALO + total + low, high - low))
        return out

    def halo(kind, s, side, to, low, there, size):
        return pltpu.make_async_remote_copy(
            src_ref=targets[kind].at[pl.ds(HALO + low, size), pl.ds(0, HDIM)],
            dst_ref=targets[kind].at[pl.ds(there, size), pl.ds(0, HDIM)],
            send_sem=halo_send.at[kind, side, s],
            recv_sem=halo_recv.at[kind, side, s],
            device_id={"ctx": to},
            device_id_type=MESH,
        )

    for kind in (K, V):
        for s in range(n):
            arrived(kind, s)
            for side, sends, _, to, low, there, size in halo_copies(s):
                @pl.when(sends)
                def _():
                    halo(kind, s, side, to, low, there, size).start()

    for kind in (K, V):
        for s in range(n):
            for side, _, gets, to, low, there, size in halo_copies(s):
                @pl.when(gets)
                def _():
                    halo(kind, s, side, to, low, there, size).wait_recv()

    factor = HDIM ** (-0.5) * math.log2(math.e)

    def attend(g):
        size = group * TILE
        span = size + 2 * HALO - TILE
        first = pl.multiple_of(g * size, TILE)
        scores = lax.dot_general(
            qa[pl.ds(first, size), :], ka[pl.ds(first, span), :],
            (((1,), (1,)), ((), ())), preferred_element_type=jnp.float32,
        )
        highest = jnp.max(scores, axis=1, keepdims=True)
        weights = jnp.exp2((scores - highest) * factor).astype(jnp.bfloat16)
        mixed = jnp.dot(weights, va[pl.ds(first, span), :], preferred_element_type=jnp.float32)
        oscr[pl.ds(first, size), :] = (mixed[:, :HDIM] / mixed[:, HDIM:]).astype(jnp.bfloat16)

    def o_rows(s):
        return oscr.at[pl.ds(pl.multiple_of(s * rows, 16), rows), :]

    def give(d):
        s = partner(me, d, n)
        return pltpu.make_async_remote_copy(
            src_ref=o_rows(s),
            dst_ref=out_ref.at[:, columns(me)],
            send_sem=o_send.at[d],
            recv_sem=o_recv.at[me],
            device_id={"head": s},
            device_id_type=MESH,
        )

    keep = pltpu.make_async_copy(o_rows(me), out_ref.at[:, columns(me)], own_sem)
    if rows == group * TILE:
        for d in range(n):
            s = partner(me, d, n)
            arrived(Q, s)
            attend(s)
            if d:
                give(d).start()
            else:
                keep.start()
    else:
        for s in range(n):
            arrived(Q, s)

        def step(g, carry):
            attend(g)
            return carry

        lax.fori_loop(0, tiles // group, step, 0)
        for d in range(1, n):
            give(d).start()
        keep.start()

    for kind in (K, V, Q):
        for d in order:
            send(kind, d).wait_send()
    for kind in (K, V):
        for s in range(n):
            for side, sends, _, to, low, there, size in halo_copies(s):
                @pl.when(sends)
                def _():
                    halo(kind, s, side, to, low, there, size).wait_send()
    keep.wait()
    for d in range(1, n):
        s = partner(me, d, n)
        there = out_ref.at[:, columns(s)]
        give(d).wait_send()
        pltpu.make_async_copy(there, there, o_recv.at[s]).wait()


def on_device(n, ctx_count, queries, keys, values, tile_lists, live_counts):
    tiles = tile_lists.shape[0]
    total = tiles * TILE
    window = total + 2 * HALO
    group = 3 if tiles % 3 == 0 else 1
    dma = pltpu.SemaphoreType.DMA
    return pl.pallas_call(
        functools.partial(kernel, n, ctx_count, tiles, group),
        out_shape=jax.ShapeDtypeStruct(queries.shape, jnp.bfloat16),
        in_specs=[
            pl.BlockSpec(memory_space=pltpu.SMEM),
            pl.BlockSpec(memory_space=pltpu.VMEM),
            pl.BlockSpec(memory_space=pl.ANY),
            pl.BlockSpec(memory_space=pl.ANY),
            pl.BlockSpec(memory_space=pl.ANY),
        ],
        out_specs=pl.BlockSpec(memory_space=pl.ANY),
        scratch_shapes=[
            pltpu.VMEM((total, 2 * HDIM), jnp.bfloat16),
            pltpu.VMEM((window, 2 * HDIM), jnp.bfloat16),
            pltpu.VMEM((window, 2 * HDIM), jnp.bfloat16),
            pltpu.VMEM((total, HDIM), jnp.bfloat16),
            pltpu.VMEM((tiles, HDIM), jnp.float32),
            dma((3, n)),
            dma((3, n)),
            dma((2, 2, n)),
            dma((2, 2, n)),
            dma((n,)),
            dma((n,)),
            dma,
        ],
        compiler_params=pltpu.CompilerParams(
            collective_id=0, has_side_effects=True, vmem_limit_bytes=48 << 20
        ),
    )(live_counts, tile_lists, queries, keys, values)


def solution(mesh):
    return jax.shard_map(
        functools.partial(on_device, mesh.shape["head"], mesh.shape["ctx"]),
        mesh=mesh,
        in_specs=(
            P(("groups", "ctx", "head"), None),
            P(("groups", "ctx", "head"), None),
            P(("groups", "ctx", "head"), None),
            P(("groups", "ctx"), None),
            P(("groups", "ctx")),
        ),
        out_specs=P(("groups", "ctx", "head"), None),
        check_vma=False,
    )
```

time: 94.9 us -> 51.8 us (0.55)
  the two profiles are of different devices: /device:TPU:0 before, /device:TPU:1 now
where the time goes in v1:
time: 51.8 us; the launch traced here: 51.5 us
  Pallas kernels  46.4 us (90%)
  local copies, waits for them, and re-layouts  5.09 us (10%)
    pallas_call x1, Pallas kernels, on_device(): pl.pallas_call(functools.partial(kernel, n, ctx_count, tiles, group), out...  46.4 us
    unnamed x11, local copies, waits for them, and re-layouts  5.09 us

profile of v1, /device:TPU:1, one launch (start us, length us, event | category | flops | bytes accessed | tf_op | source)
XLA Modules:
  0.0 51.5 jit_solution(9866888883305464170)
XLA Ops:
  0.0 0.0 copy-start
  0.0 1.0 %copy-done = bf16[384,512]{1,0:T(8,128)(2,1)S(1)} copy-done((bf16[384,512]{1,0:T(8,128)(2,1)S(1)}, bf16[384,512]{1,0:T(8,128)(2,1)}, u32[]{:S(2)}) %copy-start) | copy-done | bytes 393240
  1.0 0.0 copy-start.1
  1.0 1.0 %copy-done.1 = bf16[384,512]{1,0:T(8,128)(2,1)S(1)} copy-done((bf16[384,512]{1,0:T(8,128)(2,1)S(1)}, bf16[384,512]{1,0:T(8,128)(2,1)}, u32[]{:S(2)}) %copy-start.1) | copy-done | bytes 393240
  2.0 0.0 copy-start.2
  2.0 1.0 %copy-done.2 = bf16[384,512]{1,0:T(8,128)(2,1)S(1)} copy-done((bf16[384,512]{1,0:T(8,128)(2,1)S(1)}, bf16[384,512]{1,0:T(8,128)(2,1)}, u32[]{:S(2)}) %copy-start.2) | copy-done | bytes 393240
  3.0 0.0 copy-start.3
  3.0 0.7 %copy-done.3 = s32[12,16]{1,0:T(8,128)S(1)} copy-done((s32[12,16]{1,0:T(8,128)S(1)}, s32[12,16]{1,0:T(8,128)}, u32[]{:S(2)}) %copy-start.3) | copy-done | bytes 792
  3.7 0.0 copy-start.4
  3.7 0.7 %copy-done.4 = s32[12]{0:T(128)S(1)} copy-done((s32[12]{0:T(128)S(1)}, s32[12]{0:T(128)}, u32[]{:S(2)}) %copy-start.4) | copy-done | bytes 72
  4.3 46.4 %shard_map.55 = bf16[384,512]{1,0:T(8,128)(2,1)S(1)} custom-call(s32[12]{0:T(128)S(1)} %copy-done.4, s32[12,16]{1,0:T(8,128)S(1)} %copy-done.3, bf16[384,512]{1,0:T(8,128)(2,1)S(1)} %copy-done, bf16[384,512]{1,0:T(8,128)(2,1)S(1)} %copy-done.1, bf16[384,512]{1,0:T(8,128)(2,1)S(1)} %copy-done.2), custom_call_target="tpu_custom_call" | custom-call | tf_op jit(solution)/shard_map/pallas_call | solution.py:242
  50.7 0.7 %copy.7 = bf16[384,512]{1,0:T(8,128)(2,1)} copy(bf16[384,512]{1,0:T(8,128)(2,1)S(1)} %shard_map.55) | data formatting | bytes 786432
Async XLA Ops:
  0.0 1.0 %copy-start = (bf16[384,512]{1,0:T(8,128)(2,1)S(1)}, bf16[384,512]{1,0:T(8,128)(2,1)}, u32[]{:S(2)}) copy-start(bf16[384,512]{1,0:T(8,128)(2,1)} %q_ref.1) | copy-start | bytes 1179652
  1.0 1.0 %copy-start.1 = (bf16[384,512]{1,0:T(8,128)(2,1)S(1)}, bf16[384,512]{1,0:T(8,128)(2,1)}, u32[]{:S(2)}) copy-start(bf16[384,512]{1,0:T(8,128)(2,1)} %k_ref.1) | copy-start | bytes 1179652
  2.0 1.0 %copy-start.2 = (bf16[384,512]{1,0:T(8,128)(2,1)S(1)}, bf16[384,512]{1,0:T(8,128)(2,1)}, u32[]{:S(2)}) copy-start(bf16[384,512]{1,0:T(8,128)(2,1)} %v_ref.1) | copy-start | bytes 1179652
  3.0 0.7 %copy-start.3 = (s32[12,16]{1,0:T(8,128)S(1)}, s32[12,16]{1,0:T(8,128)}, u32[]{:S(2)}) copy-start(s32[12,16]{1,0:T(8,128)} %lists_ref.1) | copy-start | bytes 2308
  3.7 0.7 %copy-start.4 = (s32[12]{0:T(128)S(1)}, s32[12]{0:T(128)}, u32[]{:S(2)}) copy-start(s32[12]{0:T(128)} %counts_ref.1) | copy-start | bytes 148

commit v2 on v1

--- a/solution.py
+++ b/solution.py
@@ -14,7 +14,7 @@
 HALO = EDGE * TILE
 MASKED = -1e30
 MESH = pl.DeviceIdType.MESH
-K, V, Q = 0, 1, 2
+K, V = 0, 1
 
 
 def partner(me, d, n):
@@ -31,15 +31,18 @@
 
 def kernel(
     n, ctx_count, tiles, group,
-    counts_ref, lists_ref, q_ref, k_ref, v_ref, out_ref,
-    qa, ka, va, oscr, bias,
-    send_sem, recv_sem, halo_send, halo_recv, o_send, o_recv, own_sem,
+    counts_in, lists_in, q_ref, k_ref, v_ref, out_ref,
+    counts_ref, lists_ref, qa, ka, va, oscr, bias,
+    send_sem, recv_sem, q_sent, q_recv, halo_send, halo_recv, o_send, o_recv, own_sem,
 ):
     rows = q_ref.shape[0]
+    staged = rows == group * TILE and n == 4
+    pieces = group if staged else 1
+    part = rows // pieces
     total = tiles * TILE
     me = lax.axis_index("head")
     c = lax.axis_index("ctx")
-    order = sorted(range(1, n), reverse=True)
+    order = list(range(1, n))
 
     barrier = pltpu.get_barrier_semaphore()
     for d in range(1, n):
@@ -56,12 +59,11 @@
     def columns(s):
         return pl.ds(pl.multiple_of(s * HDIM, HDIM), HDIM)
 
-    sources = (k_ref, v_ref, q_ref)
-    targets = (ka, va, qa)
-    firsts = (HALO, HALO, 0)
+    sources = (k_ref, v_ref)
+    targets = (ka, va)
 
     def landing(kind, s):
-        first = firsts[kind] + s * rows
+        first = HALO + s * rows
         return targets[kind].at[pl.ds(pl.multiple_of(first, 16), rows), pl.ds(0, HDIM)]
 
     def own(kind):
@@ -84,6 +86,30 @@
         there = landing(kind, s)
         pltpu.make_async_copy(there, there, recv_sem.at[kind, s]).wait()
 
+    def q_landing(s, p):
+        first = pl.multiple_of(s * rows + p * part, 16)
+        return qa.at[pl.ds(first, part), pl.ds(0, HDIM)]
+
+    def q_own(p):
+        return pltpu.make_async_copy(
+            q_ref.at[pl.ds(p * part, part), columns(me)], q_landing(me, p), q_recv.at[me, p]
+        )
+
+    def q_send(d, p):
+        s = partner(me, d, n)
+        return pltpu.make_async_remote_copy(
+            src_ref=q_ref.at[pl.ds(p * part, part), columns(s)],
+            dst_ref=q_landing(me, p),
+            send_sem=q_sent.at[d, p],
+            recv_sem=q_recv.at[me, p],
+            device_id={"head": s},
+            device_id_type=MESH,
+        )
+
+    def q_arrived(s, p):
+        there = q_landing(s, p)
+        pltpu.make_async_copy(there, there, q_recv.at[s, p]).wait()
+
     @pl.when(jnp.logical_and(c > 0, c < ctx_count - 1))
     def _():
         pl.semaphore_wait(barrier, n + 1)
@@ -92,10 +118,20 @@
     def _():
         pl.semaphore_wait(barrier, n)
 
-    for kind in (K, V, Q):
+    for kind in (K, V):
         for d in order:
             send(kind, d).start()
         own(kind).start()
+    for p in range(pieces):
+        q_own(p).start()
+    if not staged:
+        for d in order:
+            q_send(d, 0).start()
+
+    counts_copy = pltpu.make_async_copy(counts_in, counts_ref, own_sem.at[1])
+    lists_copy = pltpu.make_async_copy(lists_in, lists_ref, own_sem.at[2])
+    counts_copy.start()
+    lists_copy.start()
 
     @pl.when(c == 0)
     def _():
@@ -113,6 +149,8 @@
         ka[pl.ds(t * TILE, TILE), pl.ds(HDIM, HDIM)] = jnp.where(lanes == t, 1.0, 0.0).astype(jnp.bfloat16)
     va[:, pl.ds(HDIM, HDIM)] = jnp.ones((window_tiles * TILE, HDIM), jnp.bfloat16)
 
+    counts_copy.wait()
+    lists_copy.wait()
     row = lax.broadcasted_iota(jnp.int32, (tiles, HDIM), 0)
     ids = lax.broadcasted_iota(jnp.int32, (tiles, HDIM), 1) + (c * tiles - EDGE)
     count = jnp.zeros((tiles, HDIM), jnp.int32)
@@ -149,6 +187,17 @@
             device_id_type=MESH,
         )
 
+    if staged:
+        for kind in (K, V):
+            send(kind, 2).wait_send()
+            if kind == K:
+                q_send(2, 0).start()
+                q_send(2, 1).start()
+            else:
+                q_send(2, 2).start()
+                for p in range(pieces):
+                    q_send(1, p).start()
+
     for kind in (K, V):
         for s in range(n):
             arrived(kind, s)
@@ -157,6 +206,11 @@
                 def _():
                     halo(kind, s, side, to, low, there, size).start()
 
+    if staged:
+        for p in range(pieces):
+            q_send(2, p).wait_send()
+            q_send(3, p).start()
+
     for kind in (K, V):
         for s in range(n):
             for side, _, gets, to, low, there, size in halo_copies(s):
@@ -166,10 +220,9 @@
 
     factor = HDIM ** (-0.5) * math.log2(math.e)
 
-    def attend(g):
-        size = group * TILE
+    def attend(first, size):
         span = size + 2 * HALO - TILE
-        first = pl.multiple_of(g * size, TILE)
+        first = pl.multiple_of(first, TILE)
         scores = lax.dot_general(
             qa[pl.ds(first, size), :], ka[pl.ds(first, span), :],
             (((1,), (1,)), ((), ())), preferred_element_type=jnp.float32,
@@ -179,46 +232,52 @@
         mixed = jnp.dot(weights, va[pl.ds(first, span), :], preferred_element_type=jnp.float32)
         oscr[pl.ds(first, size), :] = (mixed[:, :HDIM] / mixed[:, HDIM:]).astype(jnp.bfloat16)
 
-    def o_rows(s):
-        return oscr.at[pl.ds(pl.multiple_of(s * rows, 16), rows), :]
-
-    def give(d):
+    def give(d, p):
         s = partner(me, d, n)
         return pltpu.make_async_remote_copy(
-            src_ref=o_rows(s),
-            dst_ref=out_ref.at[:, columns(me)],
-            send_sem=o_send.at[d],
-            recv_sem=o_recv.at[me],
+            src_ref=oscr.at[pl.ds(pl.multiple_of(s * rows + p * part, 16), part), :],
+            dst_ref=out_ref.at[pl.ds(p * part, part), columns(me)],
+            send_sem=o_send.at[d, p],
+            recv_sem=o_recv.at[me, p],
             device_id={"head": s},
             device_id_type=MESH,
         )
 
-    keep = pltpu.make_async_copy(o_rows(me), out_ref.at[:, columns(me)], own_sem)
-    if rows == group * TILE:
-        for d in range(n):
+    keep = pltpu.make_async_copy(
+        oscr.at[pl.ds(pl.multiple_of(me * rows, 16), rows), :], out_ref.at[:, columns(me)],
+        own_sem.at[0],
+    )
+    if staged:
+        for d in (2, 1, 3):
             s = partner(me, d, n)
-            arrived(Q, s)
-            attend(s)
-            if d:
-                give(d).start()
-            else:
-                keep.start()
+            for p in range(pieces):
+                q_arrived(s, p)
+                attend(s * rows + p * TILE, TILE)
+                give(d, p).start()
+        for p in range(pieces):
+            q_arrived(me, p)
+        attend(me * rows, rows)
     else:
         for s in range(n):
-            arrived(Q, s)
+            q_arrived(s, 0)
 
         def step(g, carry):
-            attend(g)
+            attend(g * group * TILE, group * TILE)
             return carry
 
         lax.fori_loop(0, tiles // group, step, 0)
         for d in range(1, n):
-            give(d).start()
-        keep.start()
-
-    for kind in (K, V, Q):
+            give(d, 0).start()
+    keep.start()
+
+    for kind in (K, V):
         for d in order:
-            send(kind, d).wait_send()
+            if not (staged and d == 2):
+                send(kind, d).wait_send()
+    for d in order:
+        for p in range(pieces):
+            if not (staged and d == 2):
+                q_send(d, p).wait_send()
     for kind in (K, V):
         for s in range(n):
             for side, sends, _, to, low, there, size in halo_copies(s):
@@ -228,9 +287,10 @@
     keep.wait()
     for d in range(1, n):
         s = partner(me, d, n)
-        there = out_ref.at[:, columns(s)]
-        give(d).wait_send()
-        pltpu.make_async_copy(there, there, o_recv.at[s]).wait()
+        for p in range(pieces):
+            there = out_ref.at[pl.ds(p * part, part), columns(s)]
+            give(d, p).wait_send()
+            pltpu.make_async_copy(there, there, o_recv.at[s, p]).wait()
 
 
 def on_device(n, ctx_count, queries, keys, values, tile_lists, live_counts):
@@ -243,29 +303,33 @@
         functools.partial(kernel, n, ctx_count, tiles, group),
         out_shape=jax.ShapeDtypeStruct(queries.shape, jnp.bfloat16),
         in_specs=[
-            pl.BlockSpec(memory_space=pltpu.SMEM),
-            pl.BlockSpec(memory_space=pltpu.VMEM),
-            pl.BlockSpec(memory_space=pl.ANY),
-            pl.BlockSpec(memory_space=pl.ANY),
-            pl.BlockSpec(memory_space=pl.ANY),
+            pl.BlockSpec(memory_space=pltpu.HBM),
+            pl.BlockSpec(memory_space=pltpu.HBM),
+            pl.BlockSpec(memory_space=pltpu.HBM),
+            pl.BlockSpec(memory_space=pltpu.HBM),
+            pl.BlockSpec(memory_space=pltpu.HBM),
         ],
-        out_specs=pl.BlockSpec(memory_space=pl.ANY),
+        out_specs=pl.BlockSpec(memory_space=pltpu.HBM),
         scratch_shapes=[
+            pltpu.SMEM(live_counts.shape, jnp.int32),
+            pltpu.VMEM(tile_lists.shape, jnp.int32),
             pltpu.VMEM((total, 2 * HDIM), jnp.bfloat16),
             pltpu.VMEM((window, 2 * HDIM), jnp.bfloat16),
             pltpu.VMEM((window, 2 * HDIM), jnp.bfloat16),
             pltpu.VMEM((total, HDIM), jnp.bfloat16),
             pltpu.VMEM((tiles, HDIM), jnp.float32),
-            dma((3, n)),
-            dma((3, n)),
+            dma((2, n)),
+            dma((2, n)),
+            dma((n, group)),
+            dma((n, group)),
             dma((2, 2, n)),
             dma((2, 2, n)),
-            dma((n,)),
-            dma((n,)),
-            dma,
+            dma((n, group)),
+            dma((n, group)),
+            dma((3,)),
         ],
         compiler_params=pltpu.CompilerParams(
-            collective_id=0, has_side_effects=True, vmem_limit_bytes=48 << 20
+            collective_id=0, has_side_effects=True, vmem_limit_bytes=63 << 20
         ),
     )(live_counts, tile_lists, queries, keys, values)
 

time: 51.8 us -> 45.6 us (0.88)
  the two profiles are of different devices: /device:TPU:1 before, /device:TPU:0 now
where the time goes in v2:
time: 45.6 us; the launch traced here: 45.4 us
  Pallas kernels  43.7 us (96%)
  local copies, waits for them, and re-layouts  1.77 us (4%)
    pallas_call x1, Pallas kernels, on_device(): pl.pallas_call(functools.partial(kernel, n, ctx_count, tiles, group), out...  43.7 us
    unnamed x1, local copies, waits for them, and re-layouts  1.77 us

profile of v2, /device:TPU:0, one launch (start us, length us, event | category | flops | bytes accessed | tf_op | source)
XLA Modules:
  0.0 45.4 jit_solution(13274127026511275888)
XLA Ops:
  0.0 43.7 %shard_map.55 = bf16[384,512]{1,0:T(8,128)(2,1)} custom-call(s32[12]{0:T(128)} %counts_in.1, s32[12,16]{1,0:T(8,128)} %lists_in.1, bf16[384,512]{1,0:T(8,128)(2,1)} %q_ref.1, bf16[384,512]{1,0:T(8,128)(2,1)} %k_ref.1, bf16[384,512]{1,0:T(8,128)(2,1)} %v_ref.1), custom_call_target="tpu_custom_call" | custom-call | tf_op jit(solution)/shard_map/pallas_call | solution.py:302
  43.7 1.8 %copy.7 = bf16[384,512]{1,0:T(8,128)(2,1)} copy(bf16[384,512]{1,0:T(8,128)(2,1)} %shard_map.55) | data formatting | bytes 786432

commit v3 on v2

--- a/solution.py
+++ b/solution.py
@@ -248,15 +248,22 @@
         own_sem.at[0],
     )
     if staged:
-        for d in (2, 1, 3):
+        for d in (2, 1, 3, 0):
             s = partner(me, d, n)
+            if d in (0, 1, 2):
+                for p in range(pieces):
+                    q_arrived(s, p)
+                attend(s * rows, rows)
+                if d == 0:
+                    keep.start()
+                    continue
+                for p in range(pieces):
+                    give(d, p).start()
+                continue
             for p in range(pieces):
                 q_arrived(s, p)
                 attend(s * rows + p * TILE, TILE)
                 give(d, p).start()
-        for p in range(pieces):
-            q_arrived(me, p)
-        attend(me * rows, rows)
     else:
         for s in range(n):
             q_arrived(s, 0)
@@ -268,7 +275,7 @@
         lax.fori_loop(0, tiles // group, step, 0)
         for d in range(1, n):
             give(d, 0).start()
-    keep.start()
+        keep.start()
 
     for kind in (K, V):
         for d in order:

time: 45.6 us -> 45 us (0.987)
  Pallas kernels: 43.7 us -> 43 us
    pallas_call x1, Pallas kernels: 43.7 us -> 43 us  [on_device(): pl.pallas_call(functools.partial(kernel, n, ctx_count, tiles, group), out...]
where the time goes in v3:
time: 45 us; the launch traced here: 44.8 us
  Pallas kernels  43 us (96%)
  local copies, waits for them, and re-layouts  1.77 us (4%)
    pallas_call x1, Pallas kernels, on_device(): pl.pallas_call(functools.partial(kernel, n, ctx_count, tiles, group), out...  43 us
    unnamed x1, local copies, waits for them, and re-layouts  1.77 us

profile of v3, /device:TPU:0, one launch (start us, length us, event | category | flops | bytes accessed | tf_op | source)
XLA Modules:
  0.0 44.8 jit_solution(17838384640967889844)
XLA Ops:
  0.0 43.0 %shard_map.55 = bf16[384,512]{1,0:T(8,128)(2,1)} custom-call(s32[12]{0:T(128)} %counts_in.1, s32[12,16]{1,0:T(8,128)} %lists_in.1, bf16[384,512]{1,0:T(8,128)(2,1)} %q_ref.1, bf16[384,512]{1,0:T(8,128)(2,1)} %k_ref.1, bf16[384,512]{1,0:T(8,128)(2,1)} %v_ref.1), custom_call_target="tpu_custom_call" | custom-call | tf_op jit(solution)/shard_map/pallas_call | solution.py:309
  43.0 1.8 %copy.7 = bf16[384,512]{1,0:T(8,128)(2,1)} copy(bf16[384,512]{1,0:T(8,128)(2,1)} %shard_map.55) | data formatting | bytes 786432
